TPU v7x, 32 devices: a whole 2x2x4 slice. The times are simulated.
32 devices in a mesh: grp: 2 (over y), gx: 4 (over z), gy: 2 (over x), gz: 2 (over core).
Axes of the slice: x: 2, y: 2, z: 4, core: 2. Of those that a mesh axis runs over, the one named last changes fastest.
Arguments:
- core_tensor: float32 [6, 256, 256, 256], P('grp', 'gz', 'gx', 'gy'), parts along dimension 0, may hold values from -6 to 6
- factor_x: float32 [512, 512], P('gx', 'grp'), parts along dimension 1, may hold values from -0.375 to 0.375
- factor_y: float32 [512, 512], P('gy', 'grp'), parts along dimension 1, may hold values from -0.375 to 0.375
- factor_z: float32 [32, 256], P('grp', 'gz'), parts along dimension 0, may hold values from -0.375 to 0.375
- suspect_voxel_list: int32 [16, 1024], P(('gx', 'gy', 'gz'), 'grp'), parts along dimension 1, may hold values from 0 to 262143
Outputs:
- velocity: float32 [6, 16, 512, 512], P('grp', 'gz', 'gx', 'gy'), parts along dimension 0
- invariants: float32 [8, 8192], P('grp', ('gx', 'gy', 'gz')), parts along dimension 0
There are 2 independent parts, one for each index of `grp`. A program takes and returns all parts, laid end to end along the dimension named above; each array names one. Nothing has to cross between parts.
Inputs may be any that keep to these rules, and one draw needn't show every extreme that they name: `suspect_voxel_list`: entries may repeat within a brick's list.
All inputs are finite; a program needn't handle non-finite values.
Results may differ from a plain program's by a relative error of at most 0.0003.
Values sent between devices are 32-bit elements; how exact they have to be, the bound alone decides.
A program may use at most 64 MiB of HBM per device.

v0:
```python
import jax
import jax.numpy as jnp
from jax import lax
from jax.sharding import PartitionSpec as P

highest = lax.Precision.HIGHEST


def extended(block, sides, width):
    for axis, dim in sides:
        count = lax.axis_size(axis)
        forward = [(i, i + 1) for i in range(count - 1)]
        backward = [(target, source) for source, target in forward]
        low = lax.ppermute(
            lax.slice_in_dim(block, block.shape[dim] - width, None, axis=dim), axis, forward
        )
        high = lax.ppermute(lax.slice_in_dim(block, 0, width, axis=dim), axis, backward)
        block = jnp.concatenate([low, block, high], axis=dim)
    return block


def gradient_invariants(grad_x, grad_y, grad_z):
    jacobian = [
        [grad_x[0], grad_y[0], grad_z[0]],
        [grad_x[1], grad_y[1], grad_z[1]],
        [grad_x[2], grad_y[2], grad_z[2]],
    ]
    jacobian_trace_p = -(jacobian[0][0] + jacobian[1][1] + jacobian[2][2])
    square_trace = jacobian[0][0] * jacobian[0][0]
    for first in range(3):
        for second in range(3):
            if first + second > 0:
                square_trace = square_trace + jacobian[first][second] * jacobian[second][first]
    jacobian_minor_q = 0.5 * (jacobian_trace_p * jacobian_trace_p - square_trace)
    determinant = (
        jacobian[0][0] * (jacobian[1][1] * jacobian[2][2] - jacobian[1][2] * jacobian[2][1])
        - jacobian[0][1] * (jacobian[1][0] * jacobian[2][2] - jacobian[1][2] * jacobian[2][0])
        + jacobian[0][2] * (jacobian[1][0] * jacobian[2][1] - jacobian[1][1] * jacobian[2][0])
    )
    jacobian_volume_r = -determinant
    eigen_sort_test = (
        jacobian_minor_q * jacobian_minor_q * jacobian_minor_q
        + 6.75 * jacobian_volume_r * jacobian_volume_r
    )
    return jnp.stack([jacobian_trace_p, jacobian_minor_q, jacobian_volume_r, eigen_sort_test])


def shards(core_tensor, factor_x, factor_y, factor_z, suspect_voxel_list):
    partial_z = jnp.einsum(
        "kg,cgab->ckab",
        factor_z,
        core_tensor,
        precision=highest,
        preferred_element_type=jnp.float32,
    )
    slab_sum = lax.psum_scatter(partial_z, "gz", scatter_dimension=1, tiled=True)
    comps, planes = (slab_sum.shape[0], slab_sum.shape[1])
    columns = factor_y
    middle = jnp.einsum(
        "jb,ckab->ckaj",
        columns,
        lax.all_gather(slab_sum, "gy", axis=3, tiled=True),
        precision=highest,
        preferred_element_type=jnp.float32,
    )
    columns = factor_x
    field_ext = jnp.einsum(
        "ia,ckaj->ckij",
        columns,
        lax.all_gather(middle, "gx", axis=2, tiled=True),
        precision=highest,
        preferred_element_type=jnp.float32,
    )
    padded = extended(field_ext, (("gx", 2), ("gy", 3), ("gz", 1)), 1)
    cells_x = field_ext.shape[2]
    cells_y = field_ext.shape[3]
    y_step_length = padded.shape[3]
    stride_z = padded.shape[2] * padded.shape[3]
    unrolled_vector = padded.reshape(comps, -1)
    cell_list = suspect_voxel_list[0]
    plane = cell_list // (cells_x * cells_y)
    row_x = cell_list // cells_y % cells_x
    col_y = cell_list % cells_y
    centre = (plane + 1) * stride_z + (row_x + 1) * y_step_length + (col_y + 1)

    def sample_at(offset):
        return jnp.take(unrolled_vector, centre + offset, axis=1)

    grad_x = 0.5 * (sample_at(y_step_length) - sample_at(-y_step_length))
    grad_y = 0.5 * (sample_at(1) - sample_at(-1))
    grad_z = 0.5 * (sample_at(stride_z) - sample_at(-stride_z))
    return (field_ext, gradient_invariants(grad_x, grad_y, grad_z))


def solution(mesh):
    placed = (
        P("grp", "gz", "gx", "gy"),
        P("gx", "grp"),
        P("gy", "grp"),
        P("grp", "gz"),
        P(("gx", "gy", "gz"), "grp"),
    )
    return jax.shard_map(
        shards,
        mesh=mesh,
        in_specs=placed,
        out_specs=(P("grp", "gz", "gx", "gy"), P("grp", ("gx", "gy", "gz"))),
        check_vma=False,
    )
```

profile of v0, /device:TPU:0, one launch (start us, length us, event | category | flops | bytes accessed | tf_op | source)
XLA Modules:
  0.0 276.2 jit_solution(1825891829575831214)
XLA Ops:
  7.2 0.0 copy-start
  7.2 0.0 reduce-scatter.2.cloned.1.call-start
  7.2 17.2 %fusion = f32[3,64,128,16]{2,3,1,0:T(8,128)S(1)} fusion(f32[3,128,64,128]{3,2,1,0:T(8,128)} %param.7, f32[16,128]{1,0:T(8,128)} %param.10), kind=kOutput, calls=%fused_computation.6 | convolution fusion | flops 603979776 | bytes 14163968 | tf_op jit(solution)/shard_map/kg,cgab->ckab/dot_general | solution.py:49
  24.5 1.6 copy.26
  26.1 0.0 reduce-scatter.2.cloned.1.call-update
  26.1 0.0 all-gather.3.cloned.1.call-start
  26.2 11.9 %reduce-scatter.2.cloned.1.call-done = f32[3,8,64,128]{3,2,0,1:T(8,128)} async-done(((f32[3,16,64,128]{3,2,0,1:T(8,128)}), f32[3,8,64,128]{3,2,0,1:T(8,128)}) %reduce-scatter.2.cloned.1.call-update) | async-done | bytes 786448 | tf_op jit(solution)/shard_map/reduce_scatter | solution.py:56
  38.0 0.0 all-gather.3.cloned.1.call-update
  38.0 0.0 all-gather.5.cloned.1.call-start
  38.1 30.0 %all-gather.3.cloned.1.call-done = f32[3,8,64,256]{3,2,0,1:T(8,128)} async-done(((f32[3,8,64,128]{3,2,0,1:T(8,128)}), f32[3,8,64,256]{3,2,0,1:T(8,128)}) %all-gather.3.cloned.1.call-update) | async-done | bytes 1572880 | tf_op jit(solution)/shard_map/all_gather | solution.py:62
  68.1 4.0 %fusion.2 = f32[3,8,64,256]{3,2,1,0:T(8,128)} fusion(f32[3,8,64,256]{3,2,0,1:T(8,128)} %all-gather.3.cloned.1.call-done, f32[256,256]{1,0:T(8,128)S(1)} %copy-done), kind=kOutput, calls=%fused_computation.11 | convolution fusion | flops 1207959552 | bytes 3407872 | tf_op jit(solution)/shard_map/jb,ckab->ckaj/dot_general | solution.py:59
  72.0 0.0 all-gather.5.cloned.1.call-update
  72.1 0.5 compare_and_fusion.5
  72.6 115.0 %all-gather.5.cloned.1.call-done = f32[3,8,256,256]{3,2,1,0:T(8,128)} async-done(((f32[3,8,64,256]{3,2,1,0:T(8,128)}), f32[3,8,256,256]{3,2,1,0:T(8,128)}) %all-gather.5.cloned.1.call-update) | async-done | bytes 6291472 | tf_op jit(solution)/shard_map/all_gather | solution.py:70
  187.6 5.7 %convolution_bitcast_fusion = f32[3,8,128,256]{3,2,1,0:T(8,128)S(1)} fusion(f32[3,8,256,256]{3,2,1,0:T(8,128)} %all-gather.5.cloned.1.call-done, f32[128,256]{1,0:T(8,128)S(1)} %copy-done.4), kind=kOutput, calls=%fused_computation.10 | convolution fusion | flops 2415919104 | bytes 9568256 | tf_op jit(solution)/shard_map/ia,ckaj->ckij/dot_general | solution.py:67
  193.2 0.0 copy-start.1
  193.3 1.3 collective-permute-start
  194.6 1.3 collective-permute-start.1
  195.9 0.6 compare_select_fusion.3
  196.5 0.0 collective-permute-done
  196.5 3.8 %collective-permute-done.1 = f32[3,8,1,256]{3,2,1,0:T(1,128)S(1)} collective-permute-done((f32[3,8,1,256]{3,2,1,0:T(1,128)S(1)}, f32[3,8,1,256]{3,2,1,0:T(1,128)S(1)}, u32[]{:S(2)}, u32[]{:S(2)}) %collective-permute-start.1) | collective-permute-done | bytes 24608 | tf_op jit(solution)/shard_map/ppermute | solution.py:17
  200.3 0.3 pad_maximum_fusion.1
  200.6 2.2 fusion.23
  202.8 2.3 copy.8
  205.2 1.3 collective-permute-start.3
  206.5 2.3 copy.7
  208.8 4.7 %collective-permute-start.2 = (f32[3,8,130,1]{2,1,3,0:T(8,128)S(1)}, f32[3,8,130,1]{2,1,3,0:T(8,128)S(1)}, u32[]{:S(2)}, u32[]{:S(2)}) collective-permute-start(f32[3,8,130,1]{2,1,3,0:T(8,128)S(1)} %copy.7), channel_id=1, source_target_pairs={{0,2},{1,3},{4,6},{5,7},{8,10},{9,11},{12,14},{13,15},{16,18},{17,... | collective-permute-start | bytes 37448 | tf_op jit(solution)/shard_map/ppermute | solution.py:14
  213.6 1.3 pad_clamp_fusion.2
  214.8 0.0 collective-permute-done.3
  214.8 1.8 copy.10
  216.6 0.0 collective-permute-done.2
  216.6 1.8 copy.9
  218.4 1.8 pad_maximum_fusion.6
  220.3 0.6 copy.11
  220.9 1.5 collective-permute-start.4
  222.4 0.6 copy.12
  223.0 1.3 collective-permute-start.5
  224.4 0.0 collective-permute-done.4
  224.4 2.5 collective-permute-done.5
  227.0 6.1 %pad_maximum_fusion = f32[3,10,130,258]{3,2,1,0:T(8,128)} fusion(f32[3,1,130,258]{3,2,1,0:T(8,128)S(1)} %copy.14, f32[3,8,130,1]{3,2,1,0:T(8,128)S(1)} %copy-done.2, f32[3,8,1,256]{3,2,1,0:T(1,128)S(1)} %collective-permute-done.1, f32[3,8,128,256]{3,2,1,0:T(8,128)S(1)} %convolution_bitcast_fusion, f32[3,8,1,256]{3,2,1,0:T(1,128)S(1)} %collective-permute-done, ...), kind=kLoop, calls=%fused_computation.8 | loop fusion | flops 6037200 | bytes 8049600 | tf_op jit(solution)/shard_map/concatenate | solution.py:18
  233.1 10.5 %reshape.12 = f32[3,335400]{1,0:T(4,128)} reshape(f32[3,10,130,258]{3,2,1,0:T(8,128)} %pad_maximum_fusion) | data formatting | bytes 8049600 | tf_op jit(solution)/shard_map/reshape | solution.py:79
  243.5 4.2 %gather_fusion.2 = f32[512,3]{0,1:T(4,128)S(1)} fusion(f32[3,335400]{1,0:T(4,128)} %reshape.12, s32[1024]{0:T(1024)S(1)} %copy-done.8), kind=kCustom, calls=%fused_computation.2.clone | custom fusion | bytes 14336 | tf_op jit(solution)/shard_map/jit(_take)/gather | solution.py:87
  247.8 4.2 %gather_fusion.3 = f32[512,3]{0,1:T(4,128)S(1)} fusion(f32[3,335400]{1,0:T(4,128)} %reshape.12, s32[1024]{0:T(1024)S(1)} %copy-done.7), kind=kCustom, calls=%fused_computation.3.clone | custom fusion | bytes 14336 | tf_op jit(solution)/shard_map/jit(_take)/gather | solution.py:87
  252.0 4.2 %gather_fusion = f32[512,3]{0,1:T(4,128)S(1)} fusion(f32[3,335400]{1,0:T(4,128)} %reshape.12, s32[1024]{0:T(1024)S(1)} %get-tuple-element.31), kind=kCustom, calls=%fused_computation.clone | custom fusion | bytes 14336 | tf_op jit(solution)/shard_map/jit(_take)/gather | solution.py:87
  256.2 4.2 %gather_fusion.1 = f32[512,3]{0,1:T(4,128)S(1)} fusion(f32[3,335400]{1,0:T(4,128)} %reshape.12, s32[1024]{0:T(1024)S(1)} %get-tuple-element.30), kind=kCustom, calls=%fused_computation.1.clone | custom fusion | bytes 14336 | tf_op jit(solution)/shard_map/jit(_take)/gather | solution.py:87
  260.5 4.2 %gather_fusion.4 = f32[512,3]{0,1:T(4,128)S(1)} fusion(f32[3,335400]{1,0:T(4,128)} %reshape.12, s32[1024]{0:T(1024)S(1)} %get-tuple-element.27), kind=kCustom, calls=%fused_computation.4.clone | custom fusion | bytes 14336 | tf_op jit(solution)/shard_map/jit(_take)/gather | solution.py:87
  264.7 4.2 %gather_fusion.5 = f32[512,3]{0,1:T(4,128)S(1)} fusion(f32[3,335400]{1,0:T(4,128)} %reshape.12, s32[1024]{0:T(1024)S(1)} %get-tuple-element.26), kind=kCustom, calls=%fused_computation.5.clone | custom fusion | bytes 14336 | tf_op jit(solution)/shard_map/jit(_take)/gather | solution.py:87
  269.1 0.6 pad_maximum_fusion.7
  (38 shorter events, 0.3 us)
Async XLA Ops:
  7.2 60.9 %copy-start = (f32[256,256]{1,0:T(8,128)S(1)}, f32[256,256]{1,0:T(8,128)}, u32[]{:S(2)}) copy-start(f32[256,256]{1,0:T(8,128)} %param.9) | copy-start | bytes 786436
  7.2 30.8 %reduce-scatter.2.cloned.1.call-start = ((), (), s32[]{:S(2)}) async-start(), calls=%async_computation.1 | async-start | bytes 2359296 | tf_op jit(solution)/shard_map/reduce_scatter | solution.py:56
  26.1 46.0 %copy-start.14 = (s32[1,512]{1,0:T(1,128)S(1)}, s32[1,512]{1,0:T(1,128)}, u32[]{:S(2)}) copy-start(s32[1,512]{1,0:T(1,128)} %param.11) | copy-start | bytes 6148
  26.1 161.5 %copy-start.4 = (f32[128,256]{1,0:T(8,128)S(1)}, f32[128,256]{1,0:T(8,128)}, u32[]{:S(2)}) copy-start(f32[128,256]{1,0:T(8,128)} %param.8) | copy-start | bytes 393220
  26.1 41.9 %all-gather.3.cloned.1.call-start = ((), (), s32[]{:S(2)}) async-start(), calls=%async_computation.2 | async-start | bytes 2359296 | tf_op jit(solution)/shard_map/all_gather | solution.py:62
  38.0 149.5 %all-gather.5.cloned.1.call-start = ((), (), s32[]{:S(2)}) async-start(), calls=%async_computation.3 | async-start | bytes 7864320 | tf_op jit(solution)/shard_map/all_gather | solution.py:70
  72.6 123.3 %copy-start.5 = (s32[512]{0:T(512)}, s32[512]{0:T(512)S(1)}, u32[]{:S(2)}) copy-start(s32[512]{0:T(512)S(1)} %get-tuple-element.7) | copy-start | bytes 6148
  193.2 33.7 %copy-start.1 = (f32[3,8,128,256]{3,2,1,0:T(8,128)}, f32[3,8,128,256]{3,2,1,0:T(8,128)S(1)}, u32[]{:S(2)}) copy-start(f32[3,8,128,256]{3,2,1,0:T(8,128)S(1)} %convolution_bitcast_fusion) | copy-start | bytes 9437188
  193.3 3.2 %collective-permute-start = (f32[3,8,1,256]{3,2,1,0:T(1,128)S(1)}, f32[3,8,1,256]{3,2,1,0:T(1,128)S(1)}, u32[]{:S(2)}, u32[]{:S(2)}) collective-permute-start(f32[3,8,1,256]{3,2,1,0:T(1,128)S(1)} %get-tuple-element.12), channel_id=1, source_target_pairs={{0,4},{4,8},{8,12},{1,5},{5,9},{9,13},{2,6},{6,10},{10,14},{3,7},{... | collective-permute-start | bytes 73736 | tf_op jit(solution)/shard_map/ppermute | solution.py:14
  194.6 5.7 %collective-permute-start.1 = (f32[3,8,1,256]{3,2,1,0:T(1,128)S(1)}, f32[3,8,1,256]{3,2,1,0:T(1,128)S(1)}, u32[]{:S(2)}, u32[]{:S(2)}) collective-permute-start(f32[3,8,1,256]{3,2,1,0:T(1,128)S(1)} %get-tuple-element.13), channel_id=1, source_target_pairs={{4,0},{8,4},{12,8},{5,1},{9,5},{13,9},{6,2},{10,6},{14,10},{7,3},{... | collective-permute-start | bytes 73736 | tf_op jit(solution)/shard_map/ppermute | solution.py:17
  205.2 9.7 %collective-permute-start.3 = (f32[3,8,130,1]{2,1,3,0:T(8,128)S(1)}, f32[3,8,130,1]{2,1,3,0:T(8,128)S(1)}, u32[]{:S(2)}, u32[]{:S(2)}) collective-permute-start(f32[3,8,130,1]{2,1,3,0:T(8,128)S(1)} %copy.8), channel_id=1, source_target_pairs={{2,0},{3,1},{6,4},{7,5},{10,8},{11,9},{14,12},{15,13},{18,16},{19,... | collective-permute-start | bytes 37448 | tf_op jit(solution)/shard_map/ppermute | solution.py:17
  208.8 7.8 %collective-permute-start.2 = (f32[3,8,130,1]{2,1,3,0:T(8,128)S(1)}, f32[3,8,130,1]{2,1,3,0:T(8,128)S(1)}, u32[]{:S(2)}, u32[]{:S(2)}) collective-permute-start(f32[3,8,130,1]{2,1,3,0:T(8,128)S(1)} %copy.7), channel_id=1, source_target_pairs={{0,2},{1,3},{4,6},{5,7},{8,10},{9,11},{12,14},{13,15},{16,18},{17,... | collective-permute-start | bytes 37448 | tf_op jit(solution)/shard_map/ppermute | solution.py:14
  218.4 5.9 %copy-start.11 = (s32[512]{0:T(512)S(1)}, s32[512]{0:T(512)}, u32[]{:S(2)}) copy-start(s32[512]{0:T(512)} %get-tuple-element.24) | copy-start | bytes 6148
  218.4 5.9 %copy-start.12 = (s32[512]{0:T(512)S(1)}, s32[512]{0:T(512)}, u32[]{:S(2)}) copy-start(s32[512]{0:T(512)} %get-tuple-element.25) | copy-start | bytes 6148
  218.4 5.9 %copy-start.9 = (s32[512]{0:T(512)S(1)}, s32[512]{0:T(512)}, u32[]{:S(2)}) copy-start(s32[512]{0:T(512)} %get-tuple-element.21) | copy-start | bytes 6148
  218.4 5.9 %copy-start.10 = (s32[512]{0:T(512)S(1)}, s32[512]{0:T(512)}, u32[]{:S(2)}) copy-start(s32[512]{0:T(512)} %get-tuple-element.22) | copy-start | bytes 6148
  218.4 5.9 %copy-start.6 = (s32[512]{0:T(512)S(1)}, s32[512]{0:T(512)}, u32[]{:S(2)}) copy-start(s32[512]{0:T(512)} %copy-done.5) | copy-start | bytes 6148
  220.3 6.7 %copy-start.2 = (f32[3,8,130,1]{3,2,1,0:T(8,128)S(1)}, f32[3,8,130,1]{3,2,1,0:T(8,128)}, u32[]{:S(2)}) copy-start(f32[3,8,130,1]{3,2,1,0:T(8,128)} %copy.10) | copy-start | bytes 37444
  220.3 6.7 %copy-start.3 = (f32[3,8,130,1]{3,2,1,0:T(8,128)S(1)}, f32[3,8,130,1]{3,2,1,0:T(8,128)}, u32[]{:S(2)}) copy-start(f32[3,8,130,1]{3,2,1,0:T(8,128)} %copy.9) | copy-start | bytes 37444
  220.9 3.5 %collective-permute-start.4 = (f32[3,1,130,258]{3,1,2,0:T(1,128)S(1)}, f32[3,1,130,258]{3,1,2,0:T(1,128)S(1)}, u32[]{:S(2)}, u32[]{:S(2)}) collective-permute-start(f32[3,1,130,258]{3,1,2,0:T(1,128)S(1)} %copy.11), channel_id=1, source_target_pairs={{0,1},{2,3},{4,5},{6,7},{8,9},{10,11},{12,13},{14,15},{16,17},{18,... | collective-permute-start | bytes 1207448 | tf_op jit(solution)/shard_map/ppermute | solution.py:14
  223.0 3.9 %collective-permute-start.5 = (f32[3,1,130,258]{3,1,2,0:T(1,128)S(1)}, f32[3,1,130,258]{3,1,2,0:T(1,128)S(1)}, u32[]{:S(2)}, u32[]{:S(2)}) collective-permute-start(f32[3,1,130,258]{3,1,2,0:T(1,128)S(1)} %copy.12), channel_id=1, source_target_pairs={{1,0},{3,2},{5,4},{7,6},{9,8},{11,10},{13,12},{15,14},{17,16},{19,... | collective-permute-start | bytes 1207448 | tf_op jit(solution)/shard_map/ppermute | solution.py:17
  233.1 10.5 %copy-start.8 = (s32[1024]{0:T(1024)S(1)}, s32[1024]{0:T(1024)}, u32[]{:S(2)}) copy-start(s32[1024]{0:T(1024)} %get-tuple-element.29) | copy-start | bytes 12292
  233.1 14.7 %copy-start.7 = (s32[1024]{0:T(1024)S(1)}, s32[1024]{0:T(1024)}, u32[]{:S(2)}) copy-start(s32[1024]{0:T(1024)} %get-tuple-element.28) | copy-start | bytes 12292
  243.5 25.4 %copy-start.13 = (pred[512]{0:T(512)(128)(4,1)S(1)}, pred[512]{0:T(512)(128)(4,1)}, u32[]{:S(2)}) copy-start(pred[512]{0:T(512)(128)(4,1)} %get-tuple-element.6) | copy-start | bytes 1540
Sparse Core Ops, SparseCore 0:
  26.2 11.7 reduce-scatter.1
  39.6 28.3 all-gather.2
  72.2 115.3 all-gather.4
where the time goes:
time: 277 us; the launch traced here: 276 us
  waiting for transfers between devices  163 us (59%)
  local copies, waits for them, and re-layouts  49.3 us (18%)
  matrix products  26.9 us (10%)
  between operations  14.1 us (5%)
  starting transfers between devices  11.5 us (4%)
  other arithmetic  11.3 us (4%)
    all_gather x1, waiting for transfers between devices, shards(): lax.all_gather(middle, 'gx', axis=2, tiled=True)  115 us
    all_gather x1, waiting for transfers between devices, shards(): lax.all_gather(slab_sum, 'gy', axis=3, tiled=True)  30 us
    gather x6, local copies, waits for them, and re-layouts, sample_at(): return jnp.take(unrolled_vector, centre + offset, axis=1)  25.4 us
    dot_general x1, matrix products, shards(): jnp.einsum('kg,cgab->ckab', factor_z, core_tensor, precision=highest, pre...  17.2 us
    reduce_scatter x1, waiting for transfers between devices, shards(): lax.psum_scatter(partial_z, 'gz', scatter_dimension=1, tiled=True)  11.9 us
    reshape x1, local copies, waits for them, and re-layouts, shards(): unrolled_vector = padded.reshape(comps, -1)  10.5 us
    ppermute x3, starting transfers between devices, extended(): lax.ppermute(lax.slice_in_dim(block, block.shape[dim] - width, None, axis...  7.48 us
    concatenate x2, other arithmetic, extended(): block = jnp.concatenate([low, block, high], axis=dim)  6.39 us
  transfers between devices with their start and end apart: 9, of which 5 were waited for; matrix products, arithmetic and copies ran while one was open for 3% of the time, Pallas kernels for 0%

commit v1 on v0

v1 whole, which is shorter than its diff:
```python
import functools

import jax
import jax.numpy as jnp
from jax import lax
from jax.experimental import pallas as pl
from jax.experimental.pallas import tpu as pltpu
from jax.sharding import PartitionSpec as P

MESH = pl.DeviceIdType.MESH
F32 = jnp.float32
BF16 = jnp.bfloat16
SUB = 8
HALVES = 2


def split(value):
    high = value.astype(BF16)
    return high, (value - high.astype(F32)).astype(BF16)


def dot(left, right):
    return jnp.dot(left, right, preferred_element_type=F32)


def dot_last(left, right):
    return lax.dot_general(left, right, (((1,), (1,)), ((), ())), preferred_element_type=F32)


def exchange_kernel(
    sizes, core_hbm, fx_ref, fy_ref, fz_ref, wide_ref, fy_halo_ref,
    core_ref, part_ref, pair_ref, slab_ref, fx_halo_ref, kron_ref, fx_ref2,
    core_sem, pair_send, pair_recv, right_send, left_send, slab_recv,
    y_send, y_recv, z_send, z_recv, edge_send, edge_recv,
):
    nx, ny, nz = sizes
    comps, ranks_z, ranks_a, ranks_b = core_ref.shape
    planes = part_ref.shape[1]
    own = planes // nz
    chunk = own // HALVES
    cells_x = fx_ref.shape[0]
    rows = wide_ref.shape[3]
    px = lax.axis_index("gx")
    py = lax.axis_index("gy")
    pz = lax.axis_index("gz")

    for c in range(comps):
        pltpu.make_async_copy(core_hbm.at[c], core_ref.at[c], core_sem.at[c]).start()

    fx_halo_ref[...] = jnp.zeros_like(fx_halo_ref)
    fy_halo_ref[...] = jnp.zeros_like(fy_halo_ref)
    wide_ref[:, :, pl.ds(own + 1 - pz, 1)] = jnp.zeros(
        (ny, comps, 1, rows, ranks_b), F32
    )

    has_left, has_right = px > 0, px < nx - 1
    below, above = py > 0, py < ny - 1
    partner = {"gz": 1 - pz}
    barrier = pltpu.get_barrier_semaphore()

    @pl.when(has_left)
    def _():
        pl.semaphore_signal(barrier, inc=1, device_id={"gx": px - 1}, device_id_type=MESH)

    @pl.when(has_right)
    def _():
        pl.semaphore_signal(barrier, inc=1, device_id={"gx": px + 1}, device_id_type=MESH)

    for step in range(1, ny):
        pl.semaphore_signal(
            barrier, inc=1, device_id={"gy": lax.rem(py + step, ny)}, device_id_type=MESH
        )
    pl.semaphore_signal(barrier, inc=1, device_id=partner, device_id_type=MESH)

    zh, zl = split(fz_ref[...])
    tall = planes * SUB
    wide = ranks_z * SUB
    spread = (
        lax.broadcasted_iota(jnp.int32, (tall, planes), 0) // SUB
        == lax.broadcasted_iota(jnp.int32, (tall, planes), 1)
    ).astype(F32).astype(BF16)
    repeat = (
        lax.broadcasted_iota(jnp.int32, (ranks_z, wide), 1) // SUB
        == lax.broadcasted_iota(jnp.int32, (ranks_z, wide), 0)
    ).astype(F32).astype(BF16)
    same = (
        lax.broadcasted_iota(jnp.int32, (tall, wide), 0) % SUB
        == lax.broadcasted_iota(jnp.int32, (tall, wide), 1) % SUB
    )
    for index, piece in enumerate((zh, zl)):
        grown = dot(dot(spread, piece).astype(BF16), repeat)
        kron_ref[index * tall : (index + 1) * tall] = jnp.where(same, grown, 0.0).astype(BF16)

    greeted = has_left.astype(jnp.int32) + has_right.astype(jnp.int32) + ny
    pl.semaphore_wait(barrier, greeted)

    edges = []
    for index, (axis, at, low, high, source, target) in enumerate((
        ("gx", px, has_left, has_right, fx_ref, fx_halo_ref),
        ("gy", py, below, above, fy_ref, fy_halo_ref),
    )):
        last = source.shape[0] - SUB
        up = pltpu.make_async_remote_copy(
            source.at[pl.ds(last, SUB)], target.at[0], edge_send.at[index, 0],
            edge_recv.at[index, 0], device_id={axis: at + 1}, device_id_type=MESH,
        )
        down = pltpu.make_async_remote_copy(
            source.at[pl.ds(0, SUB)], target.at[1], edge_send.at[index, 1],
            edge_recv.at[index, 1], device_id={axis: at - 1}, device_id_type=MESH,
        )
        pl.when(high)(up.start)
        pl.when(low)(down.start)
        edges.append((low, high, up, down))

    def pair_copy(c):
        return pltpu.make_async_remote_copy(
            part_ref.at[c, pl.ds((1 - pz) * own, own)], pair_ref.at[c], pair_send.at[c],
            pair_recv.at[c], device_id=partner, device_id_type=MESH,
        )

    def slab_copy(q, origin, sem, target):
        return pltpu.make_async_remote_copy(
            slab_ref.at[q, origin], slab_ref.at[q, origin], sem.at[q, origin],
            slab_recv.at[q, origin], device_id={"gx": target}, device_id_type=MESH,
        )

    def contract_z(c):
        pltpu.make_async_copy(core_hbm.at[c], core_ref.at[c], core_sem.at[c]).wait()

        def body(step, carry):
            first = pl.multiple_of(step * 2 * SUB, SUB)
            both = jnp.concatenate(
                [
                    core_ref[c, :, pl.ds(first + at, SUB), :].reshape(wide, ranks_b)
                    for at in (0, SUB)
                ],
                axis=1,
            )
            high, low = split(both)
            stacked = dot(kron_ref[...], high)
            out = stacked[:tall] + stacked[tall:] + dot(kron_ref[:tall], low)
            for index, at in enumerate((0, SUB)):
                part_ref[c, :, pl.ds(first + at, SUB), :] = out[
                    :, index * ranks_b : (index + 1) * ranks_b
                ].reshape(planes, SUB, ranks_b)
            return carry

        lax.fori_loop(0, ranks_a // (2 * SUB), body, 0)
        pair_copy(c).start()

    def finish_z(c):
        pair_copy(c).wait_recv()
        for half in range(HALVES):
            q = c * HALVES + half
            slab_ref[q, px] = (
                part_ref[c, pl.ds(pz * own + half * chunk, chunk)]
                + pair_ref[c, half * chunk : (half + 1) * chunk]
            )

            @pl.when(has_right)
            def _():
                slab_copy(q, px, right_send, px + 1).start()

            @pl.when(has_left)
            def _():
                slab_copy(q, px, left_send, px - 1).start()

    contract_z(0)
    for c in range(1, comps):
        contract_z(c)
        finish_z(c - 1)
    finish_z(comps - 1)

    for low, high, up, down in edges:
        pl.when(low)(up.wait_recv)
        pl.when(high)(down.wait_recv)
    tile = lax.broadcasted_iota(jnp.int32, (2 * SUB, fx_ref.shape[1]), 0)
    outer = jnp.where(
        tile == 0, fx_halo_ref[0, SUB - 1 : SUB, :],
        jnp.where(tile == 1, fx_halo_ref[1, 0:1, :], 0.0),
    )
    full = cells_x + 2 * SUB
    xh, xl = split(jnp.concatenate([fx_ref[...], outer], axis=0))
    fx_ref2[:full] = xh
    fx_ref2[full:] = xl

    def y_copy(q, step):
        c, half = q // HALVES, q % HALVES
        block = wide_ref.at[py, c, pl.ds(half * chunk, chunk)]
        return pltpu.make_async_remote_copy(
            block, block, y_send.at[q, step - 1], y_recv.at[q, step - 1],
            device_id={"gy": lax.rem(py + step, ny)}, device_id_type=MESH,
        )

    def y_arrived(q, step):
        c, half = q // HALVES, q % HALVES
        block = wide_ref.at[lax.rem(py + ny - step, ny), c, pl.ds(half * chunk, chunk)]
        return pltpu.make_async_remote_copy(
            block, block, y_send.at[q, step - 1], y_recv.at[q, step - 1],
            device_id={"gy": lax.rem(py + step, ny)}, device_id_type=MESH,
        )

    def z_copy(c, step):
        owner = lax.rem(py + ny - step, ny)
        edge = (1 - pz) * (own - 1)
        return pltpu.make_async_remote_copy(
            wide_ref.at[owner, c, edge], wide_ref.at[owner, c, own + 1 - pz],
            z_send.at[c, step], z_recv.at[c, step], device_id=partner, device_id_type=MESH,
        )

    for q in range(comps * HALVES):
        c, half = q // HALVES, q % HALVES
        for hop in range(1, nx):
            @pl.when(px >= hop)
            def _():
                slab_copy(q, px - hop, right_send, px).wait_recv()

                @pl.when(has_right)
                def _():
                    slab_copy(q, px - hop, right_send, px + 1).start()

            @pl.when(px + hop < nx)
            def _():
                slab_copy(q, px + hop, left_send, px).wait_recv()

                @pl.when(has_left)
                def _():
                    slab_copy(q, px + hop, left_send, px - 1).start()

        for k in range(0, chunk, 2):
            both = jnp.concatenate(
                [slab_ref[q, :, k + at].reshape(nx * ranks_a, ranks_b) for at in (0, 1)], axis=1
            )
            high, low = split(both)
            stacked = dot(fx_ref2[...], high)
            out = stacked[:full] + stacked[full:] + dot(fx_ref2[:full], low)
            for at in (0, 1):
                wide_ref[py, c, half * chunk + k + at] = out[
                    :rows, at * ranks_b : (at + 1) * ranks_b
                ]
        for step in range(1, ny):
            y_copy(q, step).start()
        if half == HALVES - 1:
            z_copy(c, 0).start()

    for c in range(comps):
        for step in range(1, ny):
            for half in range(HALVES):
                y_arrived(c * HALVES + half, step).wait_recv()
            z_copy(c, step).start()

    for low, high, up, down in edges:
        pl.when(high)(up.wait_send)
        pl.when(low)(down.wait_send)
    for c in range(comps):
        pair_copy(c).wait_send()
    for q in range(comps * HALVES):
        for origin in range(nx):
            @pl.when((origin <= px) & has_right)
            def _():
                slab_copy(q, origin, right_send, px + 1).wait_send()

            @pl.when((origin >= px) & has_left)
            def _():
                slab_copy(q, origin, left_send, px - 1).wait_send()
        for step in range(1, ny):
            y_copy(q, step).wait_send()
    for c in range(comps):
        for step in range(ny):
            z_copy(c, step).wait_send()
            z_copy(c, step).wait_recv()


def field_kernel(
    cells_x, cells_y, wide_ref, fy_ref, fy_halo_ref, list_ref, field_ref, inv_ref,
    rows_ref, fy_rows_ref, prod_ref,
):
    ny, comps, slots, _, ranks_b = wide_ref.shape
    own = slots - 2
    ranks = ny * ranks_b
    lanes = 128
    parts = ranks // lanes
    count = list_ref.shape[1]
    per_plane = cells_x + 2

    def joined(c, k, start, size):
        return jnp.concatenate(
            [wide_ref[y, c, k, start : start + size, :] for y in range(ny)], axis=1
        )

    for c in range(comps):
        for k in range(slots):
            spot = 0 if k == own + 1 else k + 1
            base = spot * per_plane * SUB
            inner = joined(c, k, 0, cells_x)
            outer = joined(c, k, cells_x, SUB)
            for part in range(parts):
                cut = slice(part * lanes, (part + 1) * lanes)
                lane = c * parts + part
                rows_ref[pl.ds(base + SUB + lane, cells_x, stride=SUB), :] = inner[:, cut]
                rows_ref[pl.ds(base + lane, 1), :] = outer[0:1, cut]
                rows_ref[pl.ds(base + (cells_x + 1) * SUB + lane, 1), :] = outer[1:2, cut]
    for c in range(comps):
        for part in range(parts):
            cut = slice(part * lanes, (part + 1) * lanes)
            lane = c * parts + part
            fy_rows_ref[pl.ds(SUB + lane, cells_y, stride=SUB), :] = fy_ref[:, cut]
            fy_rows_ref[pl.ds(lane, 1), :] = fy_halo_ref[0, SUB - 1 : SUB, cut]
            fy_rows_ref[pl.ds((cells_y + 1) * SUB + lane, 1), :] = fy_halo_ref[1, 0:1, cut]

    def candidate(n, carry):
        cell = list_ref[0, n]
        plane = cell // (cells_x * cells_y)
        row = cell // cells_y % cells_x
        column = cell % cells_y
        spot = (plane + 1) * per_plane + row + 1

        def at(ref, index):
            return ref[pl.ds(pl.multiple_of(index * SUB, SUB), SUB), :]

        centre = at(fy_rows_ref, column + 1)
        here = pl.ds(pl.multiple_of(n * SUB, SUB), SUB)
        prod_ref[0, here, :] = (at(rows_ref, spot + 1) - at(rows_ref, spot - 1)) * centre
        prod_ref[1, here, :] = at(rows_ref, spot) * (
            at(fy_rows_ref, column + 2) - at(fy_rows_ref, column)
        )
        prod_ref[2, here, :] = (
            at(rows_ref, spot + per_plane) - at(rows_ref, spot - per_plane)
        ) * centre
        return carry

    lax.fori_loop(0, count, candidate, 0, unroll=8)

    fh, fl = split(fy_ref[...])
    for c in range(comps):
        flat = jnp.concatenate(
            [
                wide_ref[y, c, 0:own, 0:cells_x, :].reshape(own * cells_x, ranks_b)
                for y in range(ny)
            ],
            axis=1,
        )
        high, low = split(flat)
        out = dot_last(high, fh) + dot_last(high, fl) + dot_last(low, fh)
        field_ref[c] = out.reshape(own, cells_x, cells_y)

    ones = jnp.ones((SUB * 2, lanes), F32).astype(BF16)

    def grad(c, d):
        total = prod_ref[d, pl.ds(c * parts, count, stride=SUB), :]
        for part in range(1, parts):
            total = total + prod_ref[d, pl.ds(c * parts + part, count, stride=SUB), :]
        high, low = split(total)
        return 0.5 * (dot_last(ones, high) + dot_last(ones, low))[0:1, :]

    j = [[grad(c, d) for d in range(3)] for c in range(3)]
    p = -(j[0][0] + j[1][1] + j[2][2])
    square = j[0][0] * j[0][0]
    for a in range(3):
        for b in range(3):
            if a + b > 0:
                square = square + j[a][b] * j[b][a]
    q = 0.5 * (p * p - square)
    det = (
        j[0][0] * (j[1][1] * j[2][2] - j[1][2] * j[2][1])
        - j[0][1] * (j[1][0] * j[2][2] - j[1][2] * j[2][0])
        + j[0][2] * (j[1][0] * j[2][1] - j[1][1] * j[2][0])
    )
    r = -det
    inv_ref[0:1, :] = p
    inv_ref[1:2, :] = q
    inv_ref[2:3, :] = r
    inv_ref[3:4, :] = q * q * q + 6.75 * r * r


def shards(sizes, core_tensor, factor_x, factor_y, factor_z, suspect_voxel_list):
    nx, ny, nz = sizes
    comps, ranks_z, ranks_a, ranks_b = core_tensor.shape
    planes = factor_z.shape[0]
    own = planes // nz
    chunk = own // HALVES
    cells_x, cells_y = factor_x.shape[0], factor_y.shape[0]
    ranks_x, ranks_y = factor_x.shape[1], factor_y.shape[1]
    rows = cells_x + SUB
    chunks = comps * HALVES
    count = suspect_voxel_list.shape[1]
    vmem = pl.BlockSpec(memory_space=pltpu.VMEM)
    dma = pltpu.SemaphoreType.DMA
    wide, fy_halo = pl.pallas_call(
        functools.partial(exchange_kernel, sizes),
        out_shape=(
            jax.ShapeDtypeStruct((ny, comps, own + 2, rows, ranks_b), F32),
            jax.ShapeDtypeStruct((2, SUB, ranks_y), F32),
        ),
        in_specs=[pl.BlockSpec(memory_space=pl.ANY), vmem, vmem, vmem],
        out_specs=(vmem, vmem),
        scratch_shapes=[
            pltpu.VMEM((comps, ranks_z, ranks_a, ranks_b), F32),
            pltpu.VMEM((comps, planes, ranks_a, ranks_b), F32),
            pltpu.VMEM((comps, own, ranks_a, ranks_b), F32),
            pltpu.VMEM((chunks, nx, chunk, ranks_a, ranks_b), F32),
            pltpu.VMEM((2, SUB, ranks_x), F32),
            pltpu.VMEM((2 * planes * SUB, ranks_z * SUB), BF16),
            pltpu.VMEM((2 * (cells_x + 2 * SUB), ranks_x), BF16),
            dma((comps,)),
            dma((comps,)),
            dma((comps,)),
            dma((chunks, nx)),
            dma((chunks, nx)),
            dma((chunks, nx)),
            dma((chunks, max(ny - 1, 1))),
            dma((chunks, max(ny - 1, 1))),
            dma((comps, ny)),
            dma((comps, ny)),
            dma((2, 2)),
            dma((2, 2)),
        ],
        compiler_params=pltpu.CompilerParams(
            collective_id=0, has_side_effects=True, vmem_limit_bytes=52 * 2**20
        ),
    )(core_tensor, factor_x, factor_y, factor_z)
    field, invariants = pl.pallas_call(
        functools.partial(field_kernel, cells_x, cells_y),
        out_shape=(
            jax.ShapeDtypeStruct((comps, own, cells_x, cells_y), F32),
            jax.ShapeDtypeStruct((4, count), F32),
        ),
        in_specs=[vmem, vmem, vmem, pl.BlockSpec(memory_space=pltpu.SMEM)],
        out_specs=(vmem, vmem),
        scratch_shapes=[
            pltpu.VMEM(((own + 2) * (cells_x + 2) * SUB, 128), F32),
            pltpu.VMEM(((cells_y + 2) * SUB, 128), F32),
            pltpu.VMEM((3, count * SUB, 128), F32),
        ],
        compiler_params=pltpu.CompilerParams(vmem_limit_bytes=52 * 2**20),
    )(wide, factor_y, fy_halo, suspect_voxel_list)
    return field, invariants


def solution(mesh):
    placed = (
        P("grp", "gz", "gx", "gy"),
        P("gx", "grp"),
        P("gy", "grp"),
        P("grp", "gz"),
        P(("gx", "gy", "gz"), "grp"),
    )
    sizes = (mesh.shape["gx"], mesh.shape["gy"], mesh.shape["gz"])
    return jax.shard_map(
        functools.partial(shards, sizes),
        mesh=mesh,
        in_specs=placed,
        out_specs=(P("grp", "gz", "gx", "gy"), P("grp", ("gx", "gy", "gz"))),
        check_vma=False,
    )
```

time: 277 us -> 92.1 us (0.33)
  waiting for transfers between devices: 163 us -> 0 us
  Pallas kernels: 0 us -> 88.6 us
  local copies, waits for them, and re-layouts: 49.3 us -> 2.55 us
  matrix products: 26.9 us -> 0 us
  between operations: 14.1 us -> 0.67 us
  starting transfers between devices: 11.5 us -> 0 us
  other arithmetic: 11.3 us -> 0 us
    all_gather x2 -> x0, waiting for transfers between devices: 145 us -> none  [the longest x1 115 us: shards(): lax.all_gather(middle, 'gx', axis=2, tiled=True)]
    pallas_call x0 -> x2, Pallas kernels: none -> 88.6 us  [the longest x1 74.9 us: shards(): pl.pallas_call(functools.partial(exchange_kernel, sizes), out_shape=(jax....]
    dot_general x3 -> x0, matrix products: 26.9 us -> none  [the longest x1 17.2 us: shards(): jnp.einsum('kg,cgab->ckab', factor_z, core_tensor, precision=highest, pre...]
    gather x6 -> x0, local copies, waits for them, and re-layouts: 25.4 us -> none  [sample_at(): return jnp.take(unrolled_vector, centre + offset, axis=1)]
    reduce_scatter x1 -> x0, waiting for transfers between devices: 11.9 us -> none  [shards(): lax.psum_scatter(partial_z, 'gz', scatter_dimension=1, tiled=True)]
    ppermute x6 -> x0, starting transfers between devices: 11.4 us -> none  [the longest x3 7.48 us: extended(): lax.ppermute(lax.slice_in_dim(block, block.shape[dim] - width, None, axis...]
    reshape x1 -> x0, local copies, waits for them, and re-layouts: 10.5 us -> none  [shards(): unrolled_vector = padded.reshape(comps, -1)]
    slice x6 -> x0, local copies, waits for them, and re-layouts: 8.16 us -> none  [the longest x4 5.21 us: extended(): lax.slice_in_dim(block, block.shape[dim] - width, None, axis=dim)]
  transfers between devices with their start and end apart: 9 -> 0, of which waited for: 5 -> 0; matrix products, arithmetic and copies ran while one was open for 3% -> 0% of each run, Pallas kernels for 0% -> 0%
where the time goes in v1:
time: 92.1 us; the launch traced here: 91.8 us
  Pallas kernels  88.6 us (96%)
  local copies, waits for them, and re-layouts  2.55 us (3%)
    pallas_call x1, Pallas kernels, shards(): pl.pallas_call(functools.partial(exchange_kernel, sizes), out_shape=(jax....  74.9 us
    pallas_call x1, Pallas kernels, shards(): pl.pallas_call(functools.partial(field_kernel, cells_x, cells_y), out_sha...  13.7 us
    unnamed x10, local copies, waits for them, and re-layouts  2.55 us

profile of v1, /device:TPU:0, one launch (start us, length us, event | category | flops | bytes accessed | tf_op | source)
XLA Modules:
  0.0 91.8 jit_solution(15337026916825645482)
XLA Ops:
  0.6 0.0 copy-start
  0.6 0.9 %copy-done = f32[256,256]{1,0:T(8,128)S(1)} copy-done((f32[256,256]{1,0:T(8,128)S(1)}, f32[256,256]{1,0:T(8,128)}, u32[]{:S(2)}) %copy-start) | copy-done | bytes 262168
  1.6 0.0 copy-start.2
  1.6 0.9 copy-done.2
  2.5 0.0 copy-start.3
  2.5 0.7 copy-done.3
  3.2 0.0 copy-start.1
  3.2 0.0 copy-start.4
  3.2 74.9 %shard_map.68 = (f32[2,3,10,136,128]{4,3,2,1,0:T(8,128)}, f32[2,8,256]{2,1,0:T(8,128)S(1)}) custom-call(f32[3,128,64,128]{3,2,1,0:T(8,128)} %core_hbm.1, f32[128,256]{1,0:T(8,128)S(1)} %copy-done.2, f32[256,256]{1,0:T(8,128)S(1)} %copy-done, f32[16,128]{1,0:T(8,128)S(1)} %copy-done.3), custom_call_target="tpu_custom_call" | custom-call | tf_op jit(solution)/shard_map/pallas_call | solution.py:389
  78.1 0.0 copy-done.1
  78.1 0.0 copy-done.4
  78.1 13.7 %shard_map.69 = (f32[3,8,128,256]{3,2,1,0:T(8,128)}, f32[4,512]{1,0:T(4,128)}) custom-call(f32[2,3,10,136,128]{4,3,2,1,0:T(8,128)} %get-tuple-element.4.wide_ref, f32[256,256]{1,0:T(8,128)S(1)} %copy-done.1, f32[2,8,256]{2,1,0:T(8,128)S(1)} %get-tuple-element.5.fy_halo_ref, s32[1,512]{1,0:T(1,128)S(1)} %copy-done.4), custom_call_target="tpu_custom_call" | custom-call | tf_op jit(solution)/shard_map/pallas_call | solution.py:422
Async XLA Ops:
  0.6 1.0 %copy-start = (f32[256,256]{1,0:T(8,128)S(1)}, f32[256,256]{1,0:T(8,128)}, u32[]{:S(2)}) copy-start(f32[256,256]{1,0:T(8,128)} %fy_ref.3) | copy-start | bytes 786436
  1.6 0.9 copy-start.2
  2.5 0.7 copy-start.3
  3.2 74.9 %copy-start.1 = (f32[256,256]{1,0:T(8,128)S(1)}, f32[256,256]{1,0:T(8,128)}, u32[]{:S(2)}) copy-start(f32[256,256]{1,0:T(8,128)} %fy_ref.3) | copy-start | bytes 786436
  3.2 75.0 %copy-start.4 = (s32[1,512]{1,0:T(1,128)S(1)}, s32[1,512]{1,0:T(1,128)}, u32[]{:S(2)}) copy-start(s32[1,512]{1,0:T(1,128)} %list_ref.1) | copy-start | bytes 6148

commit v2 on v1

--- a/solution.py
+++ b/solution.py
@@ -11,7 +11,8 @@
 F32 = jnp.float32
 BF16 = jnp.bfloat16
 SUB = 8
-HALVES = 2
+HALVES = 4
+AHEAD = 3
 
 
 def split(value):
@@ -28,8 +29,9 @@
 
 
 def exchange_kernel(
-    sizes, core_hbm, fx_ref, fy_ref, fz_ref, wide_ref, fy_halo_ref,
-    core_ref, part_ref, pair_ref, slab_ref, fx_halo_ref, kron_ref, fx_ref2,
+    sizes, core_hbm, fx_hbm, fy_ref, fz_hbm, wide_ref, fy_halo_ref,
+    fx_ref, fz_ref, fx_end_ref, fx_end_ref2, partial_ref, load_sem, end_send, end_recv,
+    partial_send, partial_recv, core_ref, part_ref, pair_ref, slab_ref, fx_halo_ref, kron_ref, fx_ref2,
     core_sem, pair_send, pair_recv, right_send, left_send, slab_recv,
     y_send, y_recv, z_send, z_recv, edge_send, edge_recv,
 ):
@@ -44,6 +46,12 @@
     py = lax.axis_index("gy")
     pz = lax.axis_index("gz")
 
+    loads = [
+        pltpu.make_async_copy(source, target, load_sem.at[index])
+        for index, (source, target) in enumerate(((fz_hbm, fz_ref), (fx_hbm, fx_ref)))
+    ]
+    for load in loads:
+        load.start()
     for c in range(comps):
         pltpu.make_async_copy(core_hbm.at[c], core_ref.at[c], core_sem.at[c]).start()
 
@@ -54,6 +62,12 @@
     )
 
     has_left, has_right = px > 0, px < nx - 1
+    ends = nx >= 4 and (nx - 1) * ranks_a > rows
+    if ends:
+        feeds_left, feeds_right = px > 1, px < nx - 2
+        is_first, is_last = px == 0, px == nx - 1
+    else:
+        feeds_left, feeds_right = has_left, has_right
     below, above = py > 0, py < ny - 1
     partner = {"gz": 1 - pz}
     barrier = pltpu.get_barrier_semaphore()
@@ -72,6 +86,7 @@
         )
     pl.semaphore_signal(barrier, inc=1, device_id=partner, device_id_type=MESH)
 
+    loads[0].wait()
     zh, zl = split(fz_ref[...])
     tall = planes * SUB
     wide = ranks_z * SUB
@@ -96,7 +111,7 @@
 
     edges = []
     for index, (axis, at, low, high, source, target) in enumerate((
-        ("gx", px, has_left, has_right, fx_ref, fx_halo_ref),
+        ("gx", px, has_left, has_right, fx_hbm, fx_halo_ref),
         ("gy", py, below, above, fy_ref, fy_halo_ref),
     )):
         last = source.shape[0] - SUB
@@ -111,6 +126,16 @@
         pl.when(high)(up.start)
         pl.when(low)(down.start)
         edges.append((low, high, up, down))
+
+    def end_copy(target):
+        return pltpu.make_async_remote_copy(
+            fx_hbm, fx_end_ref, end_send, end_recv, device_id={"gx": target},
+            device_id_type=MESH,
+        )
+
+    if ends:
+        pl.when(is_first)(end_copy(1).start)
+        pl.when(is_last)(end_copy(nx - 2).start)
 
     def pair_copy(c):
         return pltpu.make_async_remote_copy(
@@ -157,19 +182,24 @@
                 + pair_ref[c, half * chunk : (half + 1) * chunk]
             )
 
-            @pl.when(has_right)
-            def _():
-                slab_copy(q, px, right_send, px + 1).start()
-
-            @pl.when(has_left)
-            def _():
-                slab_copy(q, px, left_send, px - 1).start()
+    def send_own(q):
+        @pl.when(feeds_right)
+        def _():
+            slab_copy(q, px, right_send, px + 1).start()
+
+        @pl.when(feeds_left)
+        def _():
+            slab_copy(q, px, left_send, px - 1).start()
 
     contract_z(0)
     for c in range(1, comps):
         contract_z(c)
         finish_z(c - 1)
+        if c == 1:
+            for q in range(AHEAD):
+                send_own(q)
     finish_z(comps - 1)
+    loads[1].wait()
 
     for low, high, up, down in edges:
         pl.when(low)(up.wait_recv)
@@ -184,6 +214,22 @@
     fx_ref2[:full] = xh
     fx_ref2[full:] = xl
 
+    def prepare_end(row, index):
+        end_copy(px).wait_recv()
+        extra = jnp.where(tile == index, row, 0.0)
+        eh, el = split(jnp.concatenate([fx_end_ref[...], extra], axis=0))
+        fx_end_ref2[:full] = eh
+        fx_end_ref2[full:] = el
+
+    if ends:
+        @pl.when(px == 1)
+        def _():
+            prepare_end(fx_ref[0:1, :], 1)
+
+        @pl.when(px == nx - 2)
+        def _():
+            prepare_end(fx_ref[cells_x - 1 : cells_x, :], 0)
+
     def y_copy(q, step):
         c, half = q // HALVES, q % HALVES
         block = wide_ref.at[py, c, pl.ds(half * chunk, chunk)]
@@ -208,36 +254,82 @@
             z_send.at[c, step], z_recv.at[c, step], device_id=partner, device_id_type=MESH,
         )
 
+    def expand(q, factor_ref, keep, emit):
+        empty = jnp.zeros((ranks_a, ranks_b), F32)
+        for k in range(0, chunk, 2):
+            both = jnp.concatenate(
+                [
+                    jnp.concatenate(
+                        [slab_ref[q, o, k + at] if o in keep else empty for o in range(nx)], axis=0
+                    )
+                    for at in (0, 1)
+                ],
+                axis=1,
+            )
+            high, low = split(both)
+            stacked = dot(factor_ref[...], high)
+            out = stacked[:full] + stacked[full:] + dot(factor_ref[:full], low)
+            for at in (0, 1):
+                emit(k + at, out[:rows, at * ranks_b : (at + 1) * ranks_b])
+
+    def partial_copy(q, target):
+        c, half = q // HALVES, q % HALVES
+        return pltpu.make_async_remote_copy(
+            partial_ref.at[q], wide_ref.at[py, c, pl.ds(half * chunk, chunk)],
+            partial_send.at[q], partial_recv.at[q], device_id={"gx": target},
+            device_id_type=MESH,
+        )
+
+    everyone = range(nx)
     for q in range(comps * HALVES):
         c, half = q // HALVES, q % HALVES
+
+        def emit_own(k, value):
+            wide_ref[py, c, half * chunk + k] = value
+
+        def emit_more(k, value):
+            wide_ref[py, c, half * chunk + k] += value
+
+        def emit_partial(k, value):
+            partial_ref[q, k] = value
+
         for hop in range(1, nx):
-            @pl.when(px >= hop)
+            @pl.when((px >= hop) & ((px < nx - 1) if ends else True))
             def _():
                 slab_copy(q, px - hop, right_send, px).wait_recv()
 
-                @pl.when(has_right)
+                @pl.when(feeds_right)
                 def _():
                     slab_copy(q, px - hop, right_send, px + 1).start()
 
-            @pl.when(px + hop < nx)
+            @pl.when((px + hop < nx) & ((px > 0) if ends else True))
             def _():
                 slab_copy(q, px + hop, left_send, px).wait_recv()
 
-                @pl.when(has_left)
+                @pl.when(feeds_left)
                 def _():
                     slab_copy(q, px + hop, left_send, px - 1).start()
 
-        for k in range(0, chunk, 2):
-            both = jnp.concatenate(
-                [slab_ref[q, :, k + at].reshape(nx * ranks_a, ranks_b) for at in (0, 1)], axis=1
-            )
-            high, low = split(both)
-            stacked = dot(fx_ref2[...], high)
-            out = stacked[:full] + stacked[full:] + dot(fx_ref2[:full], low)
-            for at in (0, 1):
-                wide_ref[py, c, half * chunk + k + at] = out[
-                    :rows, at * ranks_b : (at + 1) * ranks_b
-                ]
+        if q + AHEAD < comps * HALVES:
+            send_own(q + AHEAD)
+        if ends:
+            for end, near in ((0, 1), (nx - 1, nx - 2)):
+                @pl.when(px == near)
+                def _():
+                    expand(q, fx_end_ref2, [o for o in everyone if o != end], emit_partial)
+                    partial_copy(q, end).start()
+
+            @pl.when(has_left & has_right)
+            def _():
+                expand(q, fx_ref2, everyone, emit_own)
+
+            for end in (0, nx - 1):
+                @pl.when(px == end)
+                def _():
+                    partial_copy(q, end).wait_recv()
+                    expand(q, fx_ref2, [end], emit_more)
+        else:
+            expand(q, fx_ref2, everyone, emit_own)
         for step in range(1, ny):
             y_copy(q, step).start()
         if half == HALVES - 1:
@@ -249,6 +341,9 @@
                 y_arrived(c * HALVES + half, step).wait_recv()
             z_copy(c, step).start()
 
+    if ends:
+        pl.when(is_first)(end_copy(1).wait_send)
+        pl.when(is_last)(end_copy(nx - 2).wait_send)
     for low, high, up, down in edges:
         pl.when(high)(up.wait_send)
         pl.when(low)(down.wait_send)
@@ -256,15 +351,20 @@
         pair_copy(c).wait_send()
     for q in range(comps * HALVES):
         for origin in range(nx):
-            @pl.when((origin <= px) & has_right)
+            @pl.when((origin <= px) & feeds_right)
             def _():
                 slab_copy(q, origin, right_send, px + 1).wait_send()
 
-            @pl.when((origin >= px) & has_left)
+            @pl.when((origin >= px) & feeds_left)
             def _():
                 slab_copy(q, origin, left_send, px - 1).wait_send()
         for step in range(1, ny):
             y_copy(q, step).wait_send()
+        if ends:
+            for end, near in ((0, 1), (nx - 1, nx - 2)):
+                @pl.when(px == near)
+                def _():
+                    partial_copy(q, end).wait_send()
     for c in range(comps):
         for step in range(ny):
             z_copy(c, step).wait_send()
@@ -392,9 +492,19 @@
             jax.ShapeDtypeStruct((ny, comps, own + 2, rows, ranks_b), F32),
             jax.ShapeDtypeStruct((2, SUB, ranks_y), F32),
         ),
-        in_specs=[pl.BlockSpec(memory_space=pl.ANY), vmem, vmem, vmem],
+        in_specs=[pl.BlockSpec(memory_space=pl.ANY)] * 4,
         out_specs=(vmem, vmem),
         scratch_shapes=[
+            pltpu.VMEM((cells_x, ranks_x), F32),
+            pltpu.VMEM((planes, ranks_z), F32),
+            pltpu.VMEM((cells_x, ranks_x), F32),
+            pltpu.VMEM((2 * (cells_x + 2 * SUB), ranks_x), BF16),
+            pltpu.VMEM((chunks, chunk, rows, ranks_b), F32),
+            dma((2,)),
+            dma,
+            dma,
+            dma((chunks,)),
+            dma((chunks,)),
             pltpu.VMEM((comps, ranks_z, ranks_a, ranks_b), F32),
             pltpu.VMEM((comps, planes, ranks_a, ranks_b), F32),
             pltpu.VMEM((comps, own, ranks_a, ranks_b), F32),

time: 92.1 us -> 95.2 us (1.034)
  Pallas kernels: 88.6 us -> 91.7 us
    pallas_call x1, Pallas kernels: 74.9 us -> 78 us  [shards(): pl.pallas_call(functools.partial(exchange_kernel, sizes), out_shape=(jax....]
where the time goes in v2:
time: 95.2 us; the launch traced here: 94.9 us
  Pallas kernels  91.7 us (96%)
  local copies, waits for them, and re-layouts  2.55 us (3%)
    pallas_call x1, Pallas kernels, shards(): pl.pallas_call(functools.partial(exchange_kernel, sizes), out_shape=(jax....  78 us
    pallas_call x1, Pallas kernels, shards(): pl.pallas_call(functools.partial(field_kernel, cells_x, cells_y), out_sha...  13.7 us
    unnamed x10, local copies, waits for them, and re-layouts  2.55 us

profile of v2, /device:TPU:0, one launch (start us, length us, event | category | flops | bytes accessed | tf_op | source)
XLA Modules:
  0.0 94.9 jit_solution(17994177689494212831)
XLA Ops:
  0.6 0.0 copy-start
  0.6 0.9 copy-done
  1.6 0.0 copy-start.2
  1.6 0.9 copy-done.2
  2.5 0.0 copy-start.3
  2.5 0.7 copy-done.3
  3.2 0.0 copy-start.1
  3.2 0.0 copy-start.4
  3.2 78.0 %shard_map.68 = (f32[2,3,10,136,128]{4,3,2,1,0:T(8,128)}, f32[2,8,256]{2,1,0:T(8,128)S(1)}) custom-call(f32[3,128,64,128]{3,2,1,0:T(8,128)} %core_hbm.1, f32[128,256]{1,0:T(8,128)S(1)} %copy-done.2, f32[256,256]{1,0:T(8,128)S(1)} %copy-done, f32[16,128]{1,0:T(8,128)S(1)} %copy-done.3), custom_call_target="tpu_custom_call" | custom-call | tf_op jit(solution)/shard_map/pallas_call | solution.py:489
  81.2 0.0 copy-done.1
  81.2 0.0 copy-done.4
  81.2 13.7 %shard_map.69 = (f32[3,8,128,256]{3,2,1,0:T(8,128)}, f32[4,512]{1,0:T(4,128)}) custom-call(f32[2,3,10,136,128]{4,3,2,1,0:T(8,128)} %get-tuple-element.4.wide_ref, f32[256,256]{1,0:T(8,128)S(1)} %copy-done.1, f32[2,8,256]{2,1,0:T(8,128)S(1)} %get-tuple-element.5.fy_halo_ref, s32[1,512]{1,0:T(1,128)S(1)} %copy-done.4), custom_call_target="tpu_custom_call" | custom-call | tf_op jit(solution)/shard_map/pallas_call | solution.py:532
Async XLA Ops:
  0.6 1.0 %copy-start = (f32[256,256]{1,0:T(8,128)S(1)}, f32[256,256]{1,0:T(8,128)}, u32[]{:S(2)}) copy-start(f32[256,256]{1,0:T(8,128)} %fy_ref.3) | copy-start | bytes 786436
  1.6 0.9 copy-start.2
  2.5 0.7 copy-start.3
  3.2 78.0 %copy-start.1 = (f32[256,256]{1,0:T(8,128)S(1)}, f32[256,256]{1,0:T(8,128)}, u32[]{:S(2)}) copy-start(f32[256,256]{1,0:T(8,128)} %fy_ref.3) | copy-start | bytes 786436
  3.2 78.0 %copy-start.4 = (s32[1,512]{1,0:T(1,128)S(1)}, s32[1,512]{1,0:T(1,128)}, u32[]{:S(2)}) copy-start(s32[1,512]{1,0:T(1,128)} %list_ref.1) | copy-start | bytes 6148

commit v3 on v2

--- a/solution.py
+++ b/solution.py
@@ -12,7 +12,8 @@
 BF16 = jnp.bfloat16
 SUB = 8
 HALVES = 4
-AHEAD = 3
+AHEAD = 4
+SKEW = 2
 
 
 def split(value):
@@ -173,6 +174,21 @@
         lax.fori_loop(0, ranks_a // (2 * SUB), body, 0)
         pair_copy(c).start()
 
+    def send_own(q):
+        @pl.when(feeds_right)
+        def _():
+            slab_copy(q, px, right_send, px + 1).start()
+
+        @pl.when(feeds_left)
+        def _():
+            slab_copy(q, px, left_send, px - 1).start()
+
+    def send_next(q):
+        if ends:
+            pl.when(has_left & has_right)(functools.partial(send_own, q))
+        else:
+            send_own(q)
+
     def finish_z(c):
         pair_copy(c).wait_recv()
         for half in range(HALVES):
@@ -181,15 +197,8 @@
                 part_ref[c, pl.ds(pz * own + half * chunk, chunk)]
                 + pair_ref[c, half * chunk : (half + 1) * chunk]
             )
-
-    def send_own(q):
-        @pl.when(feeds_right)
-        def _():
-            slab_copy(q, px, right_send, px + 1).start()
-
-        @pl.when(feeds_left)
-        def _():
-            slab_copy(q, px, left_send, px - 1).start()
+            if ends:
+                pl.when(is_first | is_last)(functools.partial(send_own, q))
 
     contract_z(0)
     for c in range(1, comps):
@@ -197,7 +206,7 @@
         finish_z(c - 1)
         if c == 1:
             for q in range(AHEAD):
-                send_own(q)
+                send_next(q)
     finish_z(comps - 1)
     loads[1].wait()
 
@@ -281,7 +290,27 @@
         )
 
     everyone = range(nx)
-    for q in range(comps * HALVES):
+    total = comps * HALVES
+    hops = nx - 2 if ends else nx - 1
+
+    def relay(q, hop):
+        @pl.when((px >= hop) & ((px < nx - 1) if ends else True))
+        def _():
+            slab_copy(q, px - hop, right_send, px).wait_recv()
+
+            @pl.when(feeds_right)
+            def _():
+                slab_copy(q, px - hop, right_send, px + 1).start()
+
+        @pl.when((px + hop < nx) & ((px > 0) if ends else True))
+        def _():
+            slab_copy(q, px + hop, left_send, px).wait_recv()
+
+            @pl.when(feeds_left)
+            def _():
+                slab_copy(q, px + hop, left_send, px - 1).start()
+
+    def consume(q):
         c, half = q // HALVES, q % HALVES
 
         def emit_own(k, value):
@@ -293,25 +322,6 @@
         def emit_partial(k, value):
             partial_ref[q, k] = value
 
-        for hop in range(1, nx):
-            @pl.when((px >= hop) & ((px < nx - 1) if ends else True))
-            def _():
-                slab_copy(q, px - hop, right_send, px).wait_recv()
-
-                @pl.when(feeds_right)
-                def _():
-                    slab_copy(q, px - hop, right_send, px + 1).start()
-
-            @pl.when((px + hop < nx) & ((px > 0) if ends else True))
-            def _():
-                slab_copy(q, px + hop, left_send, px).wait_recv()
-
-                @pl.when(feeds_left)
-                def _():
-                    slab_copy(q, px + hop, left_send, px - 1).start()
-
-        if q + AHEAD < comps * HALVES:
-            send_own(q + AHEAD)
         if ends:
             for end, near in ((0, 1), (nx - 1, nx - 2)):
                 @pl.when(px == near)
@@ -334,6 +344,16 @@
             y_copy(q, step).start()
         if half == HALVES - 1:
             z_copy(c, 0).start()
+
+    for turn in range(total + SKEW * (hops - 1)):
+        for hop in range(1, hops + 1):
+            q = turn - SKEW * (hop - 1)
+            if 0 <= q < total:
+                relay(q, hop)
+        if turn + AHEAD < total:
+            send_next(turn + AHEAD)
+        if turn >= SKEW * (hops - 1):
+            consume(turn - SKEW * (hops - 1))
 
     for c in range(comps):
         for step in range(1, ny):

time: 95.2 us -> 83 us (0.87)
  Pallas kernels: 91.7 us -> 79.5 us
    pallas_call x1, Pallas kernels: 78 us -> 65.8 us  [shards(): pl.pallas_call(functools.partial(exchange_kernel, sizes), out_shape=(jax....]
where the time goes in v3:
time: 83 us; the launch traced here: 82.8 us
  Pallas kernels  79.5 us (96%)
  local copies, waits for them, and re-layouts  2.55 us (3%)
    pallas_call x1, Pallas kernels, shards(): pl.pallas_call(functools.partial(exchange_kernel, sizes), out_shape=(jax....  65.8 us
    pallas_call x1, Pallas kernels, shards(): pl.pallas_call(functools.partial(field_kernel, cells_x, cells_y), out_sha...  13.7 us
    unnamed x10, local copies, waits for them, and re-layouts  2.55 us

profile of v3, /device:TPU:0, one launch (start us, length us, event | category | flops | bytes accessed | tf_op | source)
XLA Modules:
  0.0 82.8 jit_solution(5191737777095914196)
XLA Ops:
  0.6 0.0 copy-start
  0.6 0.9 %copy-done = f32[256,256]{1,0:T(8,128)S(1)} copy-done((f32[256,256]{1,0:T(8,128)S(1)}, f32[256,256]{1,0:T(8,128)}, u32[]{:S(2)}) %copy-start) | copy-done | bytes 262168
  1.6 0.0 copy-start.2
  1.6 0.9 %copy-done.2 = f32[128,256]{1,0:T(8,128)S(1)} copy-done((f32[128,256]{1,0:T(8,128)S(1)}, f32[128,256]{1,0:T(8,128)}, u32[]{:S(2)}) %copy-start.2) | copy-done | bytes 131096
  2.5 0.0 copy-start.3
  2.5 0.7 copy-done.3
  3.2 0.0 copy-start.1
  3.2 0.0 copy-start.4
  3.2 65.8 %shard_map.68 = (f32[2,3,10,136,128]{4,3,2,1,0:T(8,128)}, f32[2,8,256]{2,1,0:T(8,128)S(1)}) custom-call(f32[3,128,64,128]{3,2,1,0:T(8,128)} %core_hbm.1, f32[128,256]{1,0:T(8,128)S(1)} %copy-done.2, f32[256,256]{1,0:T(8,128)S(1)} %copy-done, f32[16,128]{1,0:T(8,128)S(1)} %copy-done.3), custom_call_target="tpu_custom_call" | custom-call | tf_op jit(solution)/shard_map/pallas_call | solution.py:509
  69.0 0.0 copy-done.1
  69.0 0.0 copy-done.4
  69.1 13.7 %shard_map.69 = (f32[3,8,128,256]{3,2,1,0:T(8,128)}, f32[4,512]{1,0:T(4,128)}) custom-call(f32[2,3,10,136,128]{4,3,2,1,0:T(8,128)} %get-tuple-element.4.wide_ref, f32[256,256]{1,0:T(8,128)S(1)} %copy-done.1, f32[2,8,256]{2,1,0:T(8,128)S(1)} %get-tuple-element.5.fy_halo_ref, s32[1,512]{1,0:T(1,128)S(1)} %copy-done.4), custom_call_target="tpu_custom_call" | custom-call | tf_op jit(solution)/shard_map/pallas_call | solution.py:552
Async XLA Ops:
  0.6 1.0 %copy-start = (f32[256,256]{1,0:T(8,128)S(1)}, f32[256,256]{1,0:T(8,128)}, u32[]{:S(2)}) copy-start(f32[256,256]{1,0:T(8,128)} %fy_ref.3) | copy-start | bytes 786436
  1.6 0.9 %copy-start.2 = (f32[128,256]{1,0:T(8,128)S(1)}, f32[128,256]{1,0:T(8,128)}, u32[]{:S(2)}) copy-start(f32[128,256]{1,0:T(8,128)} %fx_hbm.1) | copy-start | bytes 393220
  2.5 0.7 copy-start.3
  3.2 65.9 %copy-start.1 = (f32[256,256]{1,0:T(8,128)S(1)}, f32[256,256]{1,0:T(8,128)}, u32[]{:S(2)}) copy-start(f32[256,256]{1,0:T(8,128)} %fy_ref.3) | copy-start | bytes 786436
  3.2 65.9 %copy-start.4 = (s32[1,512]{1,0:T(1,128)S(1)}, s32[1,512]{1,0:T(1,128)}, u32[]{:S(2)}) copy-start(s32[1,512]{1,0:T(1,128)} %list_ref.1) | copy-start | bytes 6148
